TPU v7x, 128 devices: a whole 4x4x4 slice. The times are simulated.
128 devices in a mesh: slab: 32 (over x, z, core), coil: 4 (over y).
Axes of the slice: x: 4, y: 4, z: 4, core: 2. Of those that a mesh axis runs over, the one named last changes fastest.
Arguments:
- image_now: float32 [2, 2, 160, 25600], P(None, None, 'slab'), may hold values from -3 to 3
- coil_maps: bfloat16 [8, 2, 160, 25600], P('coil', None, 'slab'), may hold values from -3 to 3
- kspace: float32 [8, 2, 65536, 128], P('coil', None, 'slab'), may hold values from -6 to 6
- row_offset: float32 [2, 4194304], P(None, 'slab'), may hold values from 0 to 3
- col_offset: float32 [2, 4194304], P(None, 'slab'), may hold values from 0 to 31
- tile_index: int32 [2, 65536], P(None, 'slab'), may hold values from 0 to 7999
- block_fill: int32 [2, 65536], P(None, 'slab'), may hold values from 1 to 64, as said below
- slab_blocks: int32 [2, 32], P(None, 'slab'), may hold values from 1 to 2048, as said below
Outputs:
- image_next: float32 [2, 2, 160, 25600], P(None, None, 'slab')
Inputs may be any that keep to these rules, and one draw needn't show every extreme that they name: Block slots b of slab q with b % 2048 >= slab_blocks[s, q] are not used, whatever kspace and the offsets hold there; for every state some slab uses all 2048 slots. The first block_fill samples of a block are used; the others are ignored, whatever kspace and the offsets hold there.
All inputs are finite; a program needn't handle non-finite values.
Results may differ from a plain program's by a relative error of at most 0.0048.
Values may be sent and summed in bfloat16 or wider, within the bound.
No kernel may reach another device: no remote copies, remote signals or barrier semaphores. Data moves between devices by JAX's collectives and lax.ppermute only.
A program may use at most 512 MiB of HBM per device.

v0:
```python
import math

import jax
import jax.numpy as jnp
from jax import lax
from jax.sharding import PartitionSpec as P

IMG = 160
TX = 4
TY = 32
BLK = 64
GROUP = 256


kernel_beta = 0.5
tv_smooth = 0.01
step_size = 0.5
tv_weight = 0.2


def with_halo(block, sides, width):
    for axis, dim in sides:
        count = lax.axis_size(axis)
        forward = [(i, i + 1) for i in range(count - 1)]
        backward = [(target, source) for source, target in forward]
        low = lax.ppermute(
            lax.slice_in_dim(block, block.shape[dim] - width, None, axis=dim), axis, forward
        )
        high = lax.ppermute(lax.slice_in_dim(block, 0, width, axis=dim), axis, backward)
        block = jnp.concatenate([low, block, high], axis=dim)
    return block


def dft_table(grid_len, img_len):
    freq_idx = jnp.arange(grid_len, dtype=jnp.int32) - grid_len // 2
    pos_idx = jnp.arange(img_len, dtype=jnp.int32) - img_len // 2
    phase_int = jnp.mod(freq_idx[:, None] * pos_idx[None, :], grid_len)
    angles = phase_int.astype(jnp.float32) * (2.0 * math.pi / grid_len)
    norm_scale = 1.0 / math.sqrt(grid_len)
    cosine = jnp.cos(angles) * norm_scale
    sine_part = jnp.sin(angles) * norm_scale
    from_real = jnp.stack([cosine, sine_part], axis=1)
    from_imag = jnp.stack([-sine_part, cosine], axis=1)
    return jnp.stack([from_real, from_imag], axis=0).astype(jnp.bfloat16)


def kernel_terms(samples, rows_s, cols_s, fill_s, live_s):
    slot_pos = jnp.arange(BLK, dtype=jnp.int32)
    in_use = ((slot_pos[None, :] < fill_s[:, None]) & live_s[:, None]).astype(jnp.float32)
    row_pos = jnp.arange(TX, dtype=jnp.float32)
    col_pos = jnp.arange(TY, dtype=jnp.float32)
    weight_x = jnp.exp(-kernel_beta * (row_pos[None, None, :] - rows_s[:, :, None]) ** 2)
    weight_y = jnp.exp(-kernel_beta * (col_pos[None, None, :] - cols_s[:, :, None]) ** 2)
    values = samples.reshape(samples.shape[0], samples.shape[1], 2, BLK) * in_use[None, :, None, :]
    spread = values[..., None] * weight_x[None, :, None, :, :]
    return jnp.einsum("cgrji,gjd->gcrid", spread, weight_y, precision=lax.Precision.HIGHEST)


def forward_diff(volume, along):
    length = volume.shape[along]
    later_part = lax.slice_in_dim(volume, 1, length, axis=along)
    behind = lax.slice_in_dim(volume, 0, length - 1, axis=along)
    closing = jnp.zeros_like(lax.slice_in_dim(volume, 0, 1, axis=along))
    return jnp.concatenate([later_part - behind, closing], axis=along)


def adjoint_diff(deltas, along):
    length = deltas.shape[along]
    opening = jnp.zeros_like(lax.slice_in_dim(deltas, 0, 1, axis=along))
    return (
        jnp.concatenate([opening, lax.slice_in_dim(deltas, 0, length - 1, axis=along)], axis=along)
        - deltas
    )


def normalize_flow(deltas):
    magnitude = jnp.sqrt(deltas[:, 0] ** 2 + deltas[:, 1] ** 2 + tv_smooth)
    return deltas / magnitude[:, None]


def coil_combine(maps_part, images_part):
    maps_re = maps_part[:, 0].astype(jnp.float32)[None]
    maps_im = maps_part[:, 1].astype(jnp.float32)[None]
    real_part = images_part[:, :, :, :, 0, :]
    imag_part = images_part[:, :, :, :, 1, :]
    sum_re = jnp.sum(maps_re * real_part + maps_im * imag_part, axis=1)
    sum_im = jnp.sum(maps_re * imag_part - maps_im * real_part, axis=1)
    return jnp.stack([sum_re, sum_im], axis=1)


def per_device(
    image_now, coil_maps, kspace, row_offset, col_offset, tile_index, block_fill, slab_blocks
):
    coil_dev, states, slot_cap, _ = kspace.shape
    slab_count = lax.axis_size("slab")
    planes_img = image_now.shape[2]
    img_len = IMG
    image_vol = image_now.reshape(states, 2, planes_img, img_len, img_len)
    maps_vol = coil_maps.reshape(coil_dev, 2, planes_img, img_len, img_len)
    rows_all = row_offset.reshape(states, slot_cap, BLK)
    cols_all = col_offset.reshape(states, slot_cap, BLK)
    grid_len = 2 * img_len
    planes_grid = grid_len // slab_count
    tiles_dev = planes_grid * (grid_len // TX) * (grid_len // TY)
    transform = dft_table(grid_len, img_len)
    group_iota = jnp.arange(GROUP, dtype=jnp.int32)
    empty_grid = jnp.zeros((tiles_dev, coil_dev, 2, TX, TY), jnp.float32)
    grids = []
    for state_no in range(states):
        used_n = slab_blocks[state_no, 0]
        group_total = (used_n + GROUP - 1) // GROUP
        samples_s = kspace[:, state_no]
        rows_s = rows_all[state_no]
        cols_s = cols_all[state_no]
        fill_s = block_fill[state_no]
        tiles_s = tile_index[state_no]
        limit = used_n

        def one_group(group_no, acc_grid):
            first_slot = group_no * GROUP
            piece_k = lax.dynamic_slice_in_dim(samples_s, first_slot, GROUP, 1)
            piece_rows = lax.dynamic_slice_in_dim(rows_s, first_slot, GROUP, 0)
            piece_cols = lax.dynamic_slice_in_dim(cols_s, first_slot, GROUP, 0)
            piece_fill = lax.dynamic_slice_in_dim(fill_s, first_slot, GROUP, 0)
            piece_tiles = lax.dynamic_slice_in_dim(tiles_s, first_slot, GROUP, 0)
            live_s = first_slot + group_iota < limit
            block_terms = kernel_terms(piece_k, piece_rows, piece_cols, piece_fill, live_s)
            return acc_grid.at[piece_tiles].add(block_terms)

        grids.append(lax.fori_loop(0, group_total, one_group, empty_grid))
    grid_half = jnp.stack(grids).astype(jnp.bfloat16)
    grid_half = grid_half.reshape(
        states, planes_grid, grid_len // TX, grid_len // TY, coil_dev, 2, TX, TY
    )
    table_y = transform.reshape(2, grid_len // TY, TY, 2, img_len)
    table_x = transform.reshape(2, grid_len // TX, TX, 2, img_len)
    line_y = jnp.einsum(
        "ezabcrid,rbdsm->ezaicsm", grid_half, table_y, preferred_element_type=jnp.float32
    ).astype(jnp.bfloat16)
    line_x = jnp.einsum(
        "ezaicrm,raisn->ecznsm", line_y, table_x, preferred_element_type=jnp.float32
    ).astype(jnp.bfloat16)
    coil_images = jnp.einsum(
        "ecqxrm,rqsz->eczxsm",
        lax.all_to_all(line_x, "slab", split_axis=3, concat_axis=2, tiled=True),
        transform,
        preferred_element_type=jnp.float32,
    )
    images_slab = lax.all_to_all(coil_images, "slab", split_axis=2, concat_axis=3, tiled=True)
    partial_sum = coil_combine(maps_vol, images_slab)
    data_grad = lax.psum(partial_sum, "coil")
    padded = with_halo(image_vol.astype(jnp.bfloat16), (("slab", 2),), 1).astype(image_vol.dtype)
    first_plane = lax.axis_index("slab") * planes_img
    plane_pos = first_plane - 1 + jnp.arange(planes_img + 1, dtype=jnp.int32)
    plane_ok = ((plane_pos >= 0) & (plane_pos <= img_len - 2)).astype(jnp.float32)
    depth_delta = (padded[:, :, 1:] - padded[:, :, :-1]) * plane_ok[None, None, :, None, None]
    depth_flow = normalize_flow(depth_delta)
    tv_grad = depth_flow[:, :, :-1] - depth_flow[:, :, 1:]
    for along in (0, 3, 4):
        tv_grad = tv_grad + adjoint_diff(normalize_flow(forward_diff(image_vol, along)), along)
    result = image_vol - step_size * (data_grad + tv_weight * tv_grad)
    return result.reshape(states, 2, planes_img, img_len * img_len)


def solution(mesh):
    return jax.shard_map(
        per_device,
        mesh=mesh,
        in_specs=(
            P(None, None, "slab", None),
            P("coil", None, "slab", None),
            P("coil", None, "slab", None),
            P(None, "slab"),
            P(None, "slab"),
            P(None, "slab"),
            P(None, "slab"),
            P(None, "slab"),
        ),
        out_specs=P(None, None, "slab", None),
        check_vma=False,
    )
```

profile of v0, /device:TPU:1, one launch (start us, length us, event | category | flops | bytes accessed | tf_op | source)
XLA Modules:
  0.0 1331.7 jit_solution(6184066912777785170)
XLA Ops:
  10.9 9.0 slice_reduce_fusion.2
  28.0 20.7 %broadcast_in_dim.6.clone.1 = f32[8000,2,2,4,32]{4,3,2,1,0:T(4,128)} broadcast(f32[]{:T(128)} %constant.95.clone.1), dimensions={} | broadcast | bytes 16384004 | tf_op jit(solution)/shard_map/broadcast_in_dim | solution.py:107
  48.7 41.5 %while.22 = (s32[]{:T(128)}, f32[8000,2,2,4,32]{4,3,2,1,0:T(4,128)}, s32[]{:T(128)}, s32[2048]{0:T(1024)S(1)}, f32[2,2048,128]{1,2,0:T(8,128)}, /*index=5*/s32[2...) while((s32[]{:T(128)}, ...), condition=%wide.region_2.3_spmd.clone, body=%wide.region_0.2_spmd.clone.sunk | while | flops 102941960 | bytes 4987587 | solution.py:130
  60.5 29.6 %scatter_fusion = f32[8000,2,2,4,32]{4,3,2,1,0:T(4,128)} fusion(f32[8000,2,2,4,32]{4,3,2,1,0:T(4,128)} %get-tuple-element.403, s32[256]{0:T(256)S(1)} %compare_select_fusion.4, f32[256,2,2,4,32]{4,3,2,1,0:T(4,128)S(1)} %fusion.146), kind=kCustom, calls=%fused_computation.clone.clone.1 | custom fusion | flops 131072 | bytes 1573888 | tf_op jit(solution)/shard_map/while/body/scatter-add | solution.py:128
  90.2 32.3 %convert.63 = bf16[8000,2,2,4,32]{4,3,2,1,0:T(4,128)(2,1)} convert(f32[8000,2,2,4,32]{4,3,2,1,0:T(4,128)} %get-tuple-element.111) | non-fusion elementwise | flops 4096000 | bytes 24576000 | tf_op jit(solution)/shard_map/convert.5
  122.5 48.7 %copy.87 = bf16[1,10,80,10,2,2,4,32]{2,7,5,3,6,4,1,0:T(8,128)(2,1)} copy(bf16[1,10,80,10,2,2,4,32]{7,6,5,4,3,2,1,0:T(4,128)(2,1)} %bitcast.157) | data formatting | bytes 16384000 | tf_op jit(solution)/shard_map/stack | solution.py:131
  175.4 20.7 %broadcast_in_dim.6.clone = f32[8000,2,2,4,32]{4,3,2,1,0:T(4,128)} broadcast(f32[]{:T(128)} %constant.95.clone.1), dimensions={} | broadcast | bytes 16384004 | tf_op jit(solution)/shard_map/broadcast_in_dim | solution.py:107
  196.1 41.9 %while.23 = (s32[]{:T(128)}, f32[8000,2,2,4,32]{4,3,2,1,0:T(4,128)}, s32[]{:T(128)}, s32[2048]{0:T(1024)S(1)}, f32[2,2048,128]{1,2,0:T(8,128)}, /*index=5*/s32[2...) while((s32[]{:T(128)}, ...), condition=%wide.region_5.6_spmd.clone, body=%wide.region_3.5_spmd.clone.sunk | while | flops 102941960 | bytes 4987587 | solution.py:130
  208.3 29.6 %scatter_fusion.1 = f32[8000,2,2,4,32]{4,3,2,1,0:T(4,128)} fusion(f32[8000,2,2,4,32]{4,3,2,1,0:T(4,128)} %get-tuple-element.364, s32[256]{0:T(256)S(1)} %compare_select_fusion.5, f32[256,2,2,4,32]{4,3,2,1,0:T(4,128)S(1)} %fusion.151), kind=kCustom, calls=%fused_computation.1.clone.clone.1 | custom fusion | flops 131072 | bytes 1573888 | tf_op jit(solution)/shard_map/while/body/scatter-add | solution.py:128
  237.9 32.3 %convert.64 = bf16[8000,2,2,4,32]{4,3,2,1,0:T(4,128)(2,1)} convert(f32[8000,2,2,4,32]{4,3,2,1,0:T(4,128)} %get-tuple-element.112) | non-fusion elementwise | flops 4096000 | bytes 24576000 | tf_op jit(solution)/shard_map/convert.4
  270.2 48.6 %copy.88 = bf16[1,10,80,10,2,2,4,32]{2,7,5,3,6,4,1,0:T(8,128)(2,1)} copy(bf16[1,10,80,10,2,2,4,32]{7,6,5,4,3,2,1,0:T(4,128)(2,1)} %bitcast.158) | data formatting | bytes 16384000 | tf_op jit(solution)/shard_map/stack | solution.py:131
  322.0 22.2 %fusion.41 = bf16[2,2,10,160,2,160]{5,3,1,2,0,4:T(8,128)(2,1)} fusion(bf16[1,10,80,10,2,2,4,32]{2,7,5,3,6,4,1,0:T(8,128)(2,1)} %copy.88, bf16[1,10,80,10,2,2,4,32]{2,7,5,3,6,4,1,0:T(8,128)(2,1)} %copy.87, bf16[1,80,4,1,160]{1,4,0,2,3:T(8,128)(2,1)S(1)} %get-tuple-element.223, bf16[1,80,4,1,160]{1,4,0,2,3:T(8,128)(2,1)S(1)} %get-tuple-element.222, ...), kind=kOutput, calls=%fused_computation.60 | convolution fusion | flops 7906508800 | bytes 21094400 | tf_op jit(solution)/shard_map/ezaicrm,raisn->ecznsm/dot_general | solution.py:140
  344.2 30.7 %copy.90 = bf16[2,2,10,160,2,160]{5,1,2,0,4,3:T(2,128)(2,1)} copy(bf16[2,2,10,160,2,160]{5,3,1,2,0,4:T(8,128)(2,1)} %fusion.41) | data formatting | bytes 8192000 | tf_op jit(solution)/shard_map/convert_element_type | solution.py:142
  375.0 588.3 %all-to-all-start = ((bf16[2,2,10,160,2,160]{5,1,2,0,4,3:T(2,128)(2,1)}), bf16[2,2,10,160,2,160]{5,1,2,0,4,3:T(2,128)(2,1)}, u32[]{:S(2)}, u32[]{:S(2)}) async-start(bf16[2,2,10,160,2,160]{5,1,2,0,4,3:T(2,128)(2,1)} %copy.90), calls=%async_computation | async-start | bytes 13107200 | tf_op jit(solution)/shard_map/all_to_all | solution.py:145
  977.0 67.5 %all-to-all-done = bf16[2,2,10,160,2,160]{5,1,2,0,4,3:T(2,128)(2,1)} async-done(((bf16[2,2,10,160,2,160]{5,1,2,0,4,3:T(2,128)(2,1)}), bf16[2,2,10,160,2,160]{5,1,2,0,4,3:T(2,128)(2,1)}, u32[]{:S(2)}, u32[]{:S(2)}) %all-to-all-start) | async-done | bytes 4096032 | tf_op jit(solution)/shard_map/all_to_all | solution.py:145
  1044.5 11.0 copy.92
  1055.6 14.2 %copy.93 = bf16[2,2,320,5,2,160]{2,5,4,3,1,0:T(8,128)(2,1)} copy(bf16[2,2,320,5,2,160]{5,4,3,2,1,0:T(2,128)(2,1)} %bitcast.162) | data formatting | bytes 8192000 | tf_op jit(solution)/shard_map/all_to_all | solution.py:145
  1077.7 10.7 copy.94
  1088.4 21.4 %all-to-all-start.1 = ((f32[2,2,160,5,2,160]{5,4,3,1,0,2:T(2,128)}), f32[2,2,160,5,2,160]{5,4,3,1,0,2:T(2,128)}, u32[]{:S(2)}, u32[]{:S(2)}) async-start(f32[2,2,160,5,2,160]{5,4,3,1,0,2:T(2,128)} %copy.94), calls=%async_computation.1 | async-start | bytes 13107200 | tf_op jit(solution)/shard_map/all_to_all | solution.py:149
  1132.1 58.9 %all-to-all-done.1 = f32[2,2,160,5,2,160]{5,4,3,1,0,2:T(2,128)} async-done(((f32[2,2,160,5,2,160]{5,4,3,1,0,2:T(2,128)}), f32[2,2,160,5,2,160]{5,4,3,1,0,2:T(2,128)}, u32[]{:S(2)}, u32[]{:S(2)}) %all-to-all-start.1) | async-done | bytes 4096032 | tf_op jit(solution)/shard_map/all_to_all | solution.py:149
  1191.0 9.1 copy.96
  1200.1 9.9 fusion.126
  1226.1 80.6 %all-reduce.8.cloned.1.call-done = f32[2,2,5,160,160]{4,3,1,2,0:T(8,128)} async-done(((f32[2,2,5,160,160]{4,3,1,2,0:T(8,128)}), f32[2,2,5,160,160]{4,3,1,2,0:T(8,128)}) %all-reduce.8.cloned.1.call-update) | async-done | bytes 2048016 | tf_op jit(solution)/shard_map/psum | solution.py:151
  1306.7 12.5 fusion.53
  (96 shorter events, 107.4 us)
Async XLA Ops:
  26.1 1.8 copy-start.10
  26.1 1.9 copy-start.11
  122.5 48.7 %copy-start.8 = (f32[131072]{0:T(1024)S(1)}, f32[131072]{0:T(1024)}, u32[]{:S(2)}) copy-start(f32[131072]{0:T(1024)} %get-tuple-element.226) | copy-start | bytes 1572868
  122.5 49.9 %copy-start.7 = (f32[131072]{0:T(1024)S(1)}, f32[131072]{0:T(1024)}, u32[]{:S(2)}) copy-start(f32[131072]{0:T(1024)} %get-tuple-element.158) | copy-start | bytes 1572868
  171.2 2.4 copy-start.3
  270.2 48.6 %copy-start.9 = (s32[10,32]{1,0:T(8,128)S(1)}, s32[10,32]{1,0:T(8,128)}, u32[]{:S(2)}) copy-start(s32[10,32]{1,0:T(8,128)} %add_add_fusion) | copy-start | bytes 3844
  270.2 48.6 %copy-start.12 = (s32[160]{0:T(256)S(1)}, s32[160]{0:T(256)}, u32[]{:S(2)}) copy-start(s32[160]{0:T(256)} %iota_add_fusion.3) | copy-start | bytes 1924
  270.2 50.2 %copy-start.13 = (s32[80,4]{0,1:T(4,128)S(1)}, s32[80,4]{0,1:T(4,128)}, u32[]{:S(2)}) copy-start(s32[80,4]{0,1:T(4,128)} %add_add_fusion.1) | copy-start | bytes 3844
  375.0 669.6 %all-to-all-start = ((bf16[2,2,10,160,2,160]{5,1,2,0,4,3:T(2,128)(2,1)}), bf16[2,2,10,160,2,160]{5,1,2,0,4,3:T(2,128)(2,1)}, u32[]{:S(2)}, u32[]{:S(2)}) async-start(bf16[2,2,10,160,2,160]{5,1,2,0,4,3:T(2,128)(2,1)} %copy.90), calls=%async_computation | async-start | bytes 13107200 | tf_op jit(solution)/shard_map/all_to_all | solution.py:145
  967.2 1.2 copy-start.1
  969.3 251.0 %collective-permute-start = (bf16[2,2,1,160,160]{4,3,1,2,0:T(8,128)(2,1)}, bf16[2,2,1,160,160]{4,3,1,2,0:T(8,128)(2,1)}, u32[]{:S(2)}, u32[]{:S(2)}) collective-permute-start(bf16[2,2,1,160,160]{4,3,1,2,0:T(8,128)(2,1)} %get-tuple-element.205), channel_id=1, source_target_pairs={{0,4},{4,8},{8,12},{12,16},{16,20},{20,24},{24,28},{28,32},{32,36}... | collective-permute-start | bytes 614408 | tf_op jit(solution)/shard_map/ppermute | solution.py:26
  972.9 247.4 %collective-permute-start.1 = (bf16[2,2,1,160,160]{4,3,1,2,0:T(8,128)(2,1)}, bf16[2,2,1,160,160]{4,3,1,2,0:T(8,128)(2,1)}, u32[]{:S(2)}, u32[]{:S(2)}) collective-permute-start(bf16[2,2,1,160,160]{4,3,1,2,0:T(8,128)(2,1)} %get-tuple-element.206), channel_id=1, source_target_pairs={{4,0},{8,4},{12,8},{16,12},{20,16},{24,20},{28,24},{32,28},{36,32}... | collective-permute-start | bytes 614408 | tf_op jit(solution)/shard_map/ppermute | solution.py:29
  1088.4 102.6 %all-to-all-start.1 = ((f32[2,2,160,5,2,160]{5,4,3,1,0,2:T(2,128)}), f32[2,2,160,5,2,160]{5,4,3,1,0,2:T(2,128)}, u32[]{:S(2)}, u32[]{:S(2)}) async-start(f32[2,2,160,5,2,160]{5,4,3,1,0,2:T(2,128)} %copy.94), calls=%async_computation.1 | async-start | bytes 13107200 | tf_op jit(solution)/shard_map/all_to_all | solution.py:149
  1109.8 196.9 %all-reduce.8.cloned.1.call-start = ((), (), s32[]{:S(2)}) async-start(), calls=%async_computation.2 | async-start | bytes 6553600 | tf_op jit(solution)/shard_map/psum | solution.py:151
  1122.9 1.4 copy-start
  1122.9 3.0 copy-start.6
  1200.1 9.9 copy-start.4
  1200.1 9.9 copy-start.5
  1217.4 2.9 copy-start.2
Sparse Core Ops, SparseCore 0:
  1213.6 93.0 all-reduce.7
where the time goes:
time: 1360 us; the launch traced here: 1330 us
  starting transfers between devices  616 us (45%)
  local copies, waits for them, and re-layouts  274 us (20%)
  waiting for transfers between devices  207 us (15%)
  other arithmetic  172 us (13%)
  matrix products  47.3 us (3%)
  between operations  15.4 us (1%)
    all_to_all x1, starting transfers between devices, per_device(): lax.all_to_all(line_x, 'slab', split_axis=3, concat_axis=2, tiled=True)  588 us
    another operation x2, local copies, waits for them, and re-layouts, per_device(): grid_half = jnp.stack(grids).astype(jnp.bfloat16)  97.2 us
    psum x1, waiting for transfers between devices, per_device(): data_grad = lax.psum(partial_sum, 'coil')  80.6 us
    another operation x5, other arithmetic  69 us
    all_to_all x1, waiting for transfers between devices, per_device(): lax.all_to_all(line_x, 'slab', split_axis=3, concat_axis=2, tiled=True)  67.5 us
    scatter-add x2, other arithmetic, one_group(): return acc_grid.at[piece_tiles].add(block_terms)  59.2 us
    all_to_all x1, waiting for transfers between devices, per_device(): lax.all_to_all(coil_images, 'slab', split_axis=2, concat_axis=3, tiled=True)  58.9 us
    broadcast_in_dim x2, local copies, waits for them, and re-layouts, per_device(): empty_grid = jnp.zeros((tiles_dev, coil_dev, 2, TX, TY), jnp.float32)  41.3 us
  transfers between devices with their start and end apart: 5, of which 3 were waited for; matrix products, arithmetic and copies ran while one was open for 8% of the time, Pallas kernels for 0%

commit v1 on v0

v1 whole, which is shorter than its diff:
```python
import math

import jax
import jax.numpy as jnp
import numpy as np
from jax import lax
from jax.experimental import pallas as pl
from jax.experimental.pallas import tpu as pltpu
from jax.sharding import PartitionSpec as P
import ml_dtypes

IMG = 160
TX = 4
TY = 32
BLK = 64
SLABS = 32

kernel_beta = 0.5
tv_smooth = 0.01
step_size = 0.5
tv_weight = 0.2

SCALE = math.sqrt(kernel_beta / math.log(2.0))
PLANES = 10
ROWS = 80
PAIRS_STEP = 8
VMEM_BYTES = 60 * 1024 * 1024


def dft_parts():
    grid_len, img_len = 2 * IMG, IMG
    freq = np.arange(grid_len) - grid_len // 2
    pos = np.arange(img_len) - img_len // 2
    angles = np.mod(freq[:, None] * pos[None, :], grid_len).astype(np.float32)
    angles = angles * np.float32(2.0 * math.pi / grid_len)
    norm = np.float32(1.0 / math.sqrt(grid_len))
    return (np.cos(angles) * norm).astype(np.float32), (np.sin(angles) * norm).astype(np.float32)


def lane_of(half, coil, m):
    j = coil * 80 + m
    return half * 128 + j if j < 128 else 256 + half * 32 + (j - 128)


def tables():
    cosine, sine = dft_parts()
    table_y = np.zeros((2, 384, 2, 384), np.float32)
    for coil in range(2):
        for half in range(2):
            for m in range(80):
                lane = lane_of(half, coil, m)
                table_y[coil, :320, 0, lane] = cosine[:, half * 80 + m]
                table_y[coil, :320, 1, lane] = sine[:, half * 80 + m]
    table_y = table_y.reshape(768, 768)
    cos_x = cosine.reshape(80, 4, 32, 5).transpose(3, 2, 0, 1)
    sin_x = sine.reshape(80, 4, 32, 5).transpose(3, 2, 0, 1)
    row_re = np.stack([cos_x, -sin_x], axis=3)
    row_im = np.stack([sin_x, cos_x], axis=3)
    table_x = np.stack([row_re, row_im]).reshape(320, 640)
    cos_z = cosine.reshape(32, 5, 2, 32, 5).transpose(4, 3, 2, 1, 0)
    sin_z = sine.reshape(32, 5, 2, 32, 5).transpose(4, 3, 2, 1, 0)
    table_z = np.stack([cos_z, sin_z]).reshape(320, 320)
    half = ml_dtypes.bfloat16
    return table_y.astype(half), table_x.astype(half), table_z.astype(half)


def grid_kernel(
    used_ref, addr_ref, fill_ref, ks_ref, row_ref, col_ref, ty_ref, tx_ref, out_ref,
    g_ref, p_ref, q_ref, s_ref,
):
    state = pl.program_id(0)
    lane = lax.broadcasted_iota(jnp.int32, (8, 128), 1)
    sub = lax.broadcasted_iota(jnp.int32, (8, 128), 0)
    left = lane < 64
    upper = sub < 4
    left_row = lax.broadcasted_iota(jnp.int32, (1, 128), 1) < 64
    col_pos = lax.broadcasted_iota(jnp.int32, (32, 128), 0).astype(jnp.float32) * SCALE
    row_pos = (sub & 3).astype(jnp.float32) * SCALE
    zero = jnp.zeros((8, 128), jnp.float32)

    def clear(i, carry):
        g_ref[pl.ds(i * 8, 8)] = jnp.zeros((8, 3, 2, 8, 128), jnp.float32)
        return carry

    lax.fori_loop(0, PLANES * ROWS // 8, clear, 0)

    def step(it, carry):
        base = it * (2 * PAIRS_STEP)
        re_rows, im_rows = [], []
        for coil in range(2):
            even = ks_ref[coil, 0, pl.ds(base, PAIRS_STEP, stride=2), :]
            odd = ks_ref[coil, 0, pl.ds(base + 1, PAIRS_STEP, stride=2), :]
            re_rows.append(jnp.where(left, even, pltpu.roll(odd, 64, 1)))
            im_rows.append(jnp.where(left, pltpu.roll(even, 64, 1), odd))
        sums, places = [], []
        for p in range(PAIRS_STEP):
            pair = it * PAIRS_STEP + p
            col_both = col_ref[pair]
            row_both = row_ref[pair]
            col = jnp.where(state == 0, col_both[0:1], col_both[1:2]) * SCALE
            row = jnp.where(state == 0, row_both[0:1], row_both[1:2]) * SCALE
            diff_y = col_pos - col
            weight_y = jnp.exp2(-(diff_y * diff_y)).astype(jnp.bfloat16)
            addr0 = addr_ref[state, base + 2 * p]
            addr1 = addr_ref[state, base + 2 * p + 1]
            spot = jnp.where(left_row, addr0 & 3, addr1 & 3)
            placed = jnp.concatenate(
                [weight_y * jnp.where(spot == b, 1.0, 0.0).astype(jnp.bfloat16) for b in range(4)],
                axis=0,
            )
            limit = jnp.where(
                left, fill_ref[state, base + 2 * p], fill_ref[state, base + 2 * p + 1] + 64
            )
            diff_x = row_pos - row
            weight_x = jnp.where(lane < limit, jnp.exp2(-(diff_x * diff_x)), 0.0)
            parts = [
                jnp.where(
                    upper,
                    jnp.broadcast_to(re_rows[coil][p : p + 1], (8, 128)),
                    jnp.broadcast_to(im_rows[coil][p : p + 1], (8, 128)),
                )
                * weight_x
                for coil in range(2)
            ]
            samples = jnp.concatenate(
                [jnp.where(left, part, zero) for part in parts]
                + [jnp.where(left, zero, part) for part in parts],
                axis=0,
            ).astype(jnp.bfloat16)
            sums.append(
                lax.dot_general(
                    samples, placed, (((1,), (1,)), ((), ())), preferred_element_type=jnp.float32
                )
            )
            places.append((addr0, addr1))
        for p in range(PAIRS_STEP):
            for which in range(2):
                addr = places[p][which]
                piece = sums[p][16 * which : 16 * which + 16].reshape(2, 8, 128)
                g_ref[addr >> 4, (addr >> 2) & 3] += piece
        return carry

    lax.fori_loop(0, (used_ref[state] + 2 * PAIRS_STEP - 1) // (2 * PAIRS_STEP), step, 0)

    def planes(pp, carry):
        tails = []
        for parity in range(2):
            plane = 2 * pp + parity
            lines = jnp.concatenate(
                [
                    g_ref[pl.ds(plane * ROWS, ROWS), quad, coil].reshape(640, 128).astype(jnp.bfloat16)
                    for coil in range(2)
                    for quad in range(3)
                ],
                axis=1,
            )
            p_ref[...] = jnp.dot(lines, ty_ref[...], preferred_element_type=jnp.float32).astype(
                jnp.bfloat16
            )
            q_ref[...] = jnp.dot(tx_ref[...], p_ref[...], preferred_element_type=jnp.float32)
            tails.append(([], []))
            for n in range(5):
                lo, hi = n * 32, 160 + n * 32
                re_part = q_ref[lo : lo + 32, 0:384] - q_ref[hi : hi + 32, 384:768]
                im_part = q_ref[hi : hi + 32, 0:384] + q_ref[lo : lo + 32, 384:768]
                for half in range(2):
                    lanes = slice(half * 128, half * 128 + 128)
                    start = (2 * parity) * 25 + n * 5
                    s_ref[half, pl.ds(start + pp, 32, stride=128), :] = re_part[:, lanes]
                    s_ref[half, pl.ds(start + 25 + pp, 32, stride=128), :] = im_part[:, lanes]
                tails[parity][0].append(re_part[:, 256:384])
                tails[parity][1].append(im_part[:, 256:384])
        lane32 = lax.broadcasted_iota(jnp.int32, (32, 128), 1)
        for n in range(5):
            pieces = [tails[0][0][n], tails[0][1][n], tails[1][0][n], tails[1][1][n]]
            for half in range(2):
                merged = None
                for place, piece in enumerate(pieces):
                    shift = (32 * (place - half)) % 128
                    moved = pltpu.roll(piece, shift, 1) if shift else piece
                    merged = (
                        moved if merged is None else jnp.where(lane32 < 32 * place, merged, moved)
                    )
                s_ref[half, pl.ds(100 + n * 5 + pp, 32, stride=128), :] = merged
        return carry

    lax.fori_loop(0, 5, planes, 0)
    for half in range(2):
        for q in range(32):
            out_ref[q, 0, half] = s_ref[half, q * 128 : q * 128 + 128, :].astype(jnp.bfloat16)


def grid_lines(used, addr, fill, kspace, rows, cols, table_y, table_x):
    return pl.pallas_call(
        grid_kernel,
        grid_spec=pltpu.PrefetchScalarGridSpec(
            num_scalar_prefetch=3,
            grid=(2,),
            in_specs=[
                pl.BlockSpec((2, 1, 2048, 128), lambda s, *_: (0, s, 0, 0)),
                pl.BlockSpec((1024, 2, 128), lambda s, *_: (0, 0, 0)),
                pl.BlockSpec((1024, 2, 128), lambda s, *_: (0, 0, 0)),
                pl.BlockSpec((768, 768), lambda s, *_: (0, 0)),
                pl.BlockSpec((320, 640), lambda s, *_: (0, 0)),
            ],
            out_specs=pl.BlockSpec((32, 1, 2, 128, 128), lambda s, *_: (0, s, 0, 0, 0)),
            scratch_shapes=[
                pltpu.VMEM((PLANES * ROWS, 3, 2, 8, 128), jnp.float32),
                pltpu.VMEM((640, 768), jnp.bfloat16),
                pltpu.VMEM((320, 768), jnp.float32),
                pltpu.VMEM((2, 32 * 128, 128), jnp.float32),
            ],
        ),
        out_shape=jax.ShapeDtypeStruct((32, 2, 2, 128, 128), jnp.bfloat16),
        compiler_params=pltpu.CompilerParams(vmem_limit_bytes=VMEM_BYTES),
        cost_estimate=pl.CostEstimate(
            flops=20_000_000_000, bytes_accessed=12_000_000, transcendentals=10_000_000
        ),
        name="grid_lines",
    )(used, addr, fill, kspace, rows, cols, table_y, table_x)


OUT_ROWS = 56


def combine_kernel(x_ref, maps_ref, tz_ref, out_ref, f_ref, t_ref):
    n = pl.program_id(0)

    @pl.when(n == 0)
    def _():
        def widen(i, carry):
            f_ref[pl.ds(i * 128, 128), :] = x_ref[i].astype(jnp.float32)
            return carry

        lax.fori_loop(0, 128, widen, 0)

    lane = lax.broadcasted_iota(jnp.int32, (160, 128), 1)
    zero = jnp.zeros((160, 128), jnp.float32)
    grad_re, grad_im, tail_re, tail_im = zero, zero, zero, zero
    for coil in range(4):

        def rows(group):
            return [
                f_ref[pl.ds(coil * 128 + group * 25 + n * 5 + pp, 32, stride=512), :]
                for pp in range(5)
            ]

        part_re = jnp.concatenate(rows(0) + rows(2), axis=0).astype(jnp.bfloat16)
        part_im = jnp.concatenate(rows(1) + rows(3), axis=0).astype(jnp.bfloat16)
        tail_rows = rows(4)
        rest = jnp.concatenate(
            tail_rows + [pltpu.roll(r, 64, 1) for r in tail_rows], axis=0
        ).astype(jnp.bfloat16)
        spread = jnp.concatenate([part_re, part_im, rest], axis=1)
        image = jnp.dot(tz_ref[...], spread, preferred_element_type=jnp.float32)
        image_re = image[:160, 0:128] - image[160:, 128:256]
        image_im = image[:160, 128:256] + image[160:, 0:128]
        map_re = maps_ref[coil, 0, 0].astype(jnp.float32)
        map_im = maps_ref[coil, 0, 1].astype(jnp.float32)
        map_tail = maps_ref[coil, 0, 2].astype(jnp.float32)
        map_swap = pltpu.roll(map_tail, 64, 1)
        grad_re = grad_re + map_re * image_re + map_im * image_im
        grad_im = grad_im + map_re * image_im - map_im * image_re
        tail_re = tail_re + image[:160, 256:] * map_tail + image[160:, 256:] * map_swap
        tail_im = tail_im + image[160:, 256:] * map_tail - image[:160, 256:] * map_swap
    for part, (grad, tail) in enumerate(((grad_re, tail_re), (grad_im, tail_im))):
        tail = tail + pltpu.roll(tail, 96, 1)
        total = grad + jnp.where(lane < 48, pltpu.roll(grad, 48, 1), pltpu.roll(tail, 48, 1))
        for z in range(5):
            t_ref[pl.ds(z * 10 + n * 2 + part, 32, stride=64), :] = total[z * 32 : z * 32 + 32]

    @pl.when(n == 4)
    def _():
        for q in range(32):
            value = t_ref[q * 64 : q * 64 + OUT_ROWS, :].astype(jnp.bfloat16)
            for copy in range(4):
                out_ref[q, copy] = value


def combine_coils(received, maps, table_z):
    return pl.pallas_call(
        combine_kernel,
        grid=(5,),
        in_specs=[
            pl.BlockSpec((128, 128, 128), lambda n: (0, 0, 0)),
            pl.BlockSpec((4, 1, 3, 160, 128), lambda n: (0, n, 0, 0, 0)),
            pl.BlockSpec((320, 320), lambda n: (0, 0)),
        ],
        out_specs=pl.BlockSpec((32, 4, OUT_ROWS, 128), lambda n: (0, 0, 0, 0)),
        out_shape=jax.ShapeDtypeStruct((32, 4, OUT_ROWS, 128), jnp.bfloat16),
        scratch_shapes=[
            pltpu.VMEM((128 * 128, 128), jnp.float32),
            pltpu.VMEM((32 * 64, 128), jnp.float32),
        ],
        compiler_params=pltpu.CompilerParams(vmem_limit_bytes=VMEM_BYTES),
        cost_estimate=pl.CostEstimate(
            flops=3_000_000_000, bytes_accessed=9_000_000, transcendentals=0
        ),
        name="combine_coils",
    )(received, maps, table_z)


def with_halo(block, sides, width):
    for axis, dim in sides:
        count = lax.axis_size(axis)
        forward = [(i, i + 1) for i in range(count - 1)]
        backward = [(target, source) for source, target in forward]
        low = lax.ppermute(
            lax.slice_in_dim(block, block.shape[dim] - width, None, axis=dim), axis, forward
        )
        high = lax.ppermute(lax.slice_in_dim(block, 0, width, axis=dim), axis, backward)
        block = jnp.concatenate([low, block, high], axis=dim)
    return block


def forward_diff(volume, along):
    length = volume.shape[along]
    later_part = lax.slice_in_dim(volume, 1, length, axis=along)
    behind = lax.slice_in_dim(volume, 0, length - 1, axis=along)
    closing = jnp.zeros_like(lax.slice_in_dim(volume, 0, 1, axis=along))
    return jnp.concatenate([later_part - behind, closing], axis=along)


def adjoint_diff(deltas, along):
    length = deltas.shape[along]
    opening = jnp.zeros_like(lax.slice_in_dim(deltas, 0, 1, axis=along))
    return (
        jnp.concatenate([opening, lax.slice_in_dim(deltas, 0, length - 1, axis=along)], axis=along)
        - deltas
    )


def normalize_flow(deltas):
    magnitude = jnp.sqrt(deltas[:, 0] ** 2 + deltas[:, 1] ** 2 + tv_smooth)
    return deltas / magnitude[:, None]


def map_pieces(coil_maps):
    maps = coil_maps.reshape(2, 2, 5, 32, 5, 2, 80)
    maps = maps.transpose(3, 5, 4, 1, 2, 0, 6).reshape(32, 2, 5, 2, 5, 160)
    main, rest = maps[..., :128], maps[..., 128:]
    rest_re, rest_im = rest[:, :, :, 0], rest[:, :, :, 1]
    tail = jnp.concatenate([rest_re, rest_im, rest_im, -rest_re], axis=-1)
    pieces = jnp.concatenate([main, tail[:, :, :, None]], axis=3)
    pieces = pieces.reshape(32, 1, 2, 75, 128)
    return jnp.broadcast_to(pieces, (32, 2, 2, 75, 128)).reshape(128, 75, 128)


def per_device(
    image_now, coil_maps, kspace, row_offset, col_offset, tile_index, block_fill, slab_blocks
):
    states = 2
    planes_img = image_now.shape[2]
    img_len = IMG
    table_y, table_x, table_z = (jnp.asarray(t) for t in tables())
    everywhere = ("slab", "coil")

    maps_sent = lax.all_to_all(map_pieces(coil_maps), everywhere, 0, 0, tiled=True)
    maps_here = maps_sent.reshape(32, 4, 5, 3, 5, 128).transpose(1, 2, 3, 4, 0, 5)
    maps_here = maps_here.reshape(4, 5, 3, 160, 128)

    slot = jnp.arange(2048, dtype=jnp.int32)
    fill = jnp.where(slot[None, :] < slab_blocks, block_fill, 0)
    addr = (tile_index // 10) * 16 + tile_index % 10
    rows = row_offset.reshape(2, 1024, 128).transpose(1, 0, 2)
    cols = col_offset.reshape(2, 1024, 128).transpose(1, 0, 2)
    lines = grid_lines(
        slab_blocks.reshape(2), addr, fill, kspace, rows, cols, table_y, table_x
    )
    received = lax.all_to_all(lines.reshape(128, 128, 128), everywhere, 0, 0, tiled=True)
    shares = combine_coils(received, maps_here, table_z)
    gathered = lax.all_to_all(
        shares.reshape(128, OUT_ROWS, 128), everywhere, 0, 0, tiled=True
    )
    grad = gathered[:, :50, :80].reshape(32, 2, 2, 5, 5, 2, 80)
    grad = grad.transpose(1, 5, 3, 0, 4, 2, 6).reshape(2, 2, planes_img, img_len * img_len)

    image_vol = image_now.reshape(states, 2, planes_img, img_len, img_len)
    padded = with_halo(image_vol.astype(jnp.bfloat16), (("slab", 2),), 1).astype(image_vol.dtype)
    first_plane = lax.axis_index("slab") * planes_img
    plane_pos = first_plane - 1 + jnp.arange(planes_img + 1, dtype=jnp.int32)
    plane_ok = ((plane_pos >= 0) & (plane_pos <= img_len - 2)).astype(jnp.float32)
    depth_delta = (padded[:, :, 1:] - padded[:, :, :-1]) * plane_ok[None, None, :, None, None]
    depth_flow = normalize_flow(depth_delta)
    tv_grad = depth_flow[:, :, :-1] - depth_flow[:, :, 1:]
    for along in (0, 3, 4):
        tv_grad = tv_grad + adjoint_diff(normalize_flow(forward_diff(image_vol, along)), along)
    base = image_vol - step_size * tv_weight * tv_grad
    base = base.reshape(states, 2, planes_img, img_len * img_len)
    return base - step_size * grad.astype(jnp.float32)


def solution(mesh):
    return jax.shard_map(
        per_device,
        mesh=mesh,
        in_specs=(
            P(None, None, "slab", None),
            P("coil", None, "slab", None),
            P("coil", None, "slab", None),
            P(None, "slab"),
            P(None, "slab"),
            P(None, "slab"),
            P(None, "slab"),
            P(None, "slab"),
        ),
        out_specs=P(None, None, "slab", None),
        check_vma=False,
    )
```

time: 1360 us -> 283 us (0.21); the launches traced: 1330 us -> 282 us
  starting transfers between devices: 616 us -> 108 us
  local copies, waits for them, and re-layouts: 274 us -> 49.7 us
  waiting for transfers between devices: 207 us -> 37.4 us
  other arithmetic: 172 us -> 32.7 us
  Pallas kernels: 0 us -> 54.1 us
  matrix products: 47.3 us -> 0 us
  between operations: 15.4 us -> 0.3 us
    all_to_all x2 -> x3, starting transfers between devices: 610 us -> 102 us  [the longest x1 85.4 us: per_device(): lax.all_to_all(lines.reshape(128, 128, 128), everywhere, 0, 0, tiled=True)]
    another operation x2 -> x0, local copies, waits for them, and re-layouts: 97.2 us -> none  [per_device(): grid_half = jnp.stack(grids).astype(jnp.bfloat16)]
    all_to_all x2 -> x3, waiting for transfers between devices: 126 us -> 37.4 us  [the longest x1 27 us: per_device(): lax.all_to_all(lines.reshape(128, 128, 128), everywhere, 0, 0, tiled=True)]
    psum x1 -> x0, waiting for transfers between devices: 80.6 us -> none  [per_device(): data_grad = lax.psum(partial_sum, 'coil')]
    another operation x7 -> x0, other arithmetic: 71.8 us -> none
    scatter-add x2 -> x0, other arithmetic: 59.2 us -> none  [one_group(): return acc_grid.at[piece_tiles].add(block_terms)]
    pallas_call x0 -> x2, Pallas kernels: none -> 54.1 us  [the longest x1 41 us: grid_lines(): pl.pallas_call(grid_kernel, grid_spec=pltpu.PrefetchScalarGridSpec(num_sc...]
    dot_general x4 -> x0, matrix products: 47.3 us -> none  [the longest x1 22.2 us: per_device(): jnp.einsum('ezaicrm,raisn->ecznsm', line_y, table_x, preferred_element_ty...]
  transfers between devices with their start and end apart: 5 -> 5, of which waited for: 3 -> 2; matrix products, arithmetic and copies ran while one was open for 8% -> 15% of each run, Pallas kernels for 0% -> 15%
where the time goes in v1:
time: 283 us; the launch traced here: 282 us
  starting transfers between devices  108 us (38%)
  Pallas kernels  54.1 us (19%)
  local copies, waits for them, and re-layouts  49.7 us (18%)
  waiting for transfers between devices  37.4 us (13%)
  other arithmetic  32.7 us (12%)
    all_to_all x1, starting transfers between devices, per_device(): lax.all_to_all(lines.reshape(128, 128, 128), everywhere, 0, 0, tiled=True)  85.4 us
    pallas_call x1, Pallas kernels, grid_lines(): pl.pallas_call(grid_kernel, grid_spec=pltpu.PrefetchScalarGridSpec(num_sc...  41 us
    all_to_all x1, waiting for transfers between devices, per_device(): lax.all_to_all(lines.reshape(128, 128, 128), everywhere, 0, 0, tiled=True)  27 us
    pallas_call x1, Pallas kernels, combine_coils(): pl.pallas_call(combine_kernel, grid=(5,), in_specs=[pl.BlockSpec((128, 12...  13.1 us
    mul x2, local copies, waits for them, and re-layouts, per_device(): return base - step_size * grad.astype(jnp.float32)  12.3 us
    all_to_all x1, starting transfers between devices, per_device(): lax.all_to_all(map_pieces(coil_maps), everywhere, 0, 0, tiled=True)  11.9 us
    div x7, other arithmetic, normalize_flow(): return deltas / magnitude[:, None]  11.6 us
    all_to_all x1, waiting for transfers between devices, per_device(): lax.all_to_all(shares.reshape(128, OUT_ROWS, 128), everywhere, 0, 0, tile...  10.4 us
  transfers between devices with their start and end apart: 5, of which 2 were waited for; matrix products, arithmetic and copies ran while one was open for 15% of the time, Pallas kernels for 15%

profile of v1, /device:TPU:1, one launch (start us, length us, event | category | flops | bytes accessed | tf_op | source)
XLA Modules:
  0.0 282.1 jit_solution(14891178842142295372)
XLA Ops:
  0.0 8.1 %reshape.83 = bf16[2,2,5,32,5,2,80]{6,5,4,3,1,2,0:T(2,128)(2,1)S(1)} reshape(bf16[2,2,5,25600]{3,1,2,0:T(2,128)(2,1)} %param.12) | data formatting | bytes 2048000 | tf_op jit(solution)/shard_map/reshape | solution.py:339
  14.3 11.9 %all-to-all-start.1 = ((bf16[128,75,128]{2,1,0:T(8,128)(2,1)}), bf16[128,75,128]{2,1,0:T(8,128)(2,1)}, u32[]{:S(2)}, u32[]{:S(2)}) async-start(bf16[128,75,128]{2,1,0:T(8,128)(2,1)} %bitcast.16), calls=%async_computation.1 | async-start | bytes 5242880 | tf_op jit(solution)/shard_map/all_to_all | solution.py:358
  26.2 3.7 %reshape.77 = f32[2,2,5,160,160]{4,3,1,2,0:T(8,128)S(1)} reshape(f32[2,2,5,25600]{3,1,2,0:T(2,128)} %param.11) | data formatting | bytes 4096000 | tf_op jit(solution)/shard_map/reshape | solution.py:378
  32.1 3.7 %collective-permute-start = (bf16[2,2,1,160,160]{4,3,1,2,0:T(8,128)(2,1)}, bf16[2,2,1,160,160]{4,3,1,2,0:T(8,128)(2,1)}, u32[]{:S(2)}, u32[]{:S(2)}) collective-permute-start(bf16[2,2,1,160,160]{4,3,1,2,0:T(8,128)(2,1)} %get-tuple-element.7), channel_id=1, source_target_pairs={{0,4},{4,8},{8,12},{12,16},{16,20},{20,24},{24,28},{28,32},{32,36}... | collective-permute-start | bytes 614408 | tf_op jit(solution)/shard_map/ppermute | solution.py:308
  35.8 2.1 collective-permute-start.1
  38.6 41.0 %grid_lines.1 = bf16[32,2,2,128,128]{4,3,2,1,0:T(8,128)(2,1)} custom-call(s32[2]{0:T(128)} %bitcast.67, s32[2,2048]{1,0:T(2,128)} %get-tuple-element.12.addr_ref, s32[2,2048]{1,0:T(2,128)} %get-tuple-element.11.fill_ref, f32[2,2,2048,128]{3,2,1,0:T(8,128)} %ks_ref.1, f32[1024,2,128]{2,1,0:T(2,128)} %bitcast.69, f32[1024,2,128]{2,1,0:T(2,128)} %bitcast.70, ...), custom_call_target="tpu_custom_call" | custom-call | flops 20000000000 | bytes 12000000 | tf_op jit(solution)/shard_map/grid_lines/pallas_call | solution.py:194
  79.6 85.4 %all-to-all-start = ((bf16[128,128,128]{2,1,0:T(8,128)(2,1)}), bf16[128,128,128]{2,1,0:T(8,128)(2,1)}, u32[]{:S(2)}, u32[]{:S(2)}) async-start(bf16[128,128,128]{2,1,0:T(8,128)(2,1)} %bitcast.64), calls=%async_computation | async-start | bytes 8388608 | tf_op jit(solution)/shard_map/all_to_all | solution.py:370
  165.0 3.1 %slice_subtract_fusion.4 = f32[1,2,5,25600]{3,1,2,0:T(2,128)} fusion(f32[2,2,5,25600]{3,1,2,0:T(2,128)} %param.11), kind=kLoop, calls=%fused_computation.48 | loop fusion | flops 256000 | bytes 3072000 | tf_op jit(solution)/shard_map/sub | solution.py:321
  168.1 3.3 %sub.54 = f32[1,2,5,160,160]{4,3,1,2,0:T(8,128)} reshape(f32[1,2,5,25600]{3,1,2,0:T(2,128)} %slice_subtract_fusion.4) | data formatting | bytes 2048000 | tf_op jit(solution)/shard_map/sub | solution.py:321
  175.2 4.0 %pad_divide_fusion.1 = (f32[2,2,5,160,160]{4,3,1,2,0:T(8,128)}, f32[2,2,5,160,160]{4,3,1,2,0:T(8,128)}) fusion(f32[2,2,5,160,159]{4,3,1,2,0:T(8,128)S(1)} %slice_subtract_fusion.1, f32[2,5,160,160]{3,2,1,0:T(8,128)S(1)} %fusion.20, f32[2,5,160,160]{3,2,1,0:T(8,128)S(1)} %fusion.14, f32[2,2,5,159,160]{4,3,1,2,0:T(8,128)S(1)} %slice_subtract_fusion.2), kind=kLoop, calls=%fused_computation.14 | loop fusion | flops 1024000 | bytes 10214400 | tf_op jit(solution)/shard_map/div | solution.py:335
  179.3 2.1 pad_divide_fusion
  181.4 2.2 maximum_convert_fusion
  183.6 2.8 fusion
  186.9 2.4 copy.32
  191.2 27.0 %all-to-all-done.x_ref = bf16[128,128,128]{2,1,0:T(8,128)(2,1)} async-done(((bf16[128,128,128]{2,1,0:T(8,128)(2,1)}), bf16[128,128,128]{2,1,0:T(8,128)(2,1)}, u32[]{:S(2)}, u32[]{:S(2)}) %all-to-all-start) | async-done | bytes 4194336 | tf_op jit(solution)/shard_map/all_to_all | solution.py:370
  218.1 13.1 %combine_coils.1 = bf16[32,4,56,128]{3,2,1,0:T(8,128)(2,1)} custom-call(bf16[128,128,128]{2,1,0:T(8,128)(2,1)} %all-to-all-done.x_ref, bf16[4,5,3,160,128]{4,3,2,1,0:T(8,128)(2,1)} %bitcast.65, bf16[320,320]{1,0:T(8,128)(2,1)} %constant.55.clone.tz_ref), custom_call_target="tpu_custom_call" | custom-call | flops 3000000000 | bytes 9000000 | tf_op jit(solution)/shard_map/combine_coils/pallas_call | solution.py:281
  231.3 4.9 %all-to-all-start.2 = ((bf16[128,56,128]{2,1,0:T(8,128)(2,1)}), bf16[128,56,128]{2,1,0:T(8,128)(2,1)}, u32[]{:S(2)}, u32[]{:S(2)}) async-start(bf16[128,56,128]{2,1,0:T(8,128)(2,1)} %bitcast.66), calls=%async_computation.2 | async-start | bytes 3670016 | tf_op jit(solution)/shard_map/all_to_all | solution.py:372
  236.2 3.0 %fusion.9 = f32[2,6,160,160]{3,2,1,0:T(8,128)S(1)} fusion(f32[2,2,6,160,160]{4,3,1,2,0:T(8,128)} %fusion), kind=kLoop, calls=%fused_computation.25 | loop fusion | flops 1228800 | bytes 3686400 | tf_op jit(solution)/shard_map/div | solution.py:335
  243.9 4.4 %fusion.5 = f32[2,2,5,160,160]{4,3,1,2,0:T(8,128)} fusion(f32[2,2,5,160,160]{4,3,1,2,0:T(8,128)S(1)} %reshape.77, f32[2,2,6,160,160]{4,3,1,2,0:T(8,128)S(1)} %broadcast_divide_fusion, f32[2,2,5,160,160]{4,3,1,2,0:T(8,128)S(1)} %copy-done.2, f32[2,2,5,160,159]{4,3,1,2,0:T(8,128)S(1)} %bitcast.58, f32[2,2,5,160,160]{4,3,1,2,0:T(8,128)S(1)} %copy-done.3, ...), kind=kLoop, calls=%fused_computation.12 | loop fusion | flops 5120000 | bytes 19430400 | tf_op jit(solution)/shard_map/sub | solution.py:388
  248.3 5.3 %reshape.78 = f32[2,2,5,25600]{3,1,2,0:T(2,128)} reshape(f32[2,2,5,160,160]{4,3,1,2,0:T(8,128)} %fusion.5) | data formatting | bytes 4096000 | tf_op jit(solution)/shard_map/reshape | solution.py:389
  253.6 10.4 %all-to-all-done.2 = bf16[128,56,128]{2,1,0:T(8,128)(2,1)} async-done(((bf16[128,56,128]{2,1,0:T(8,128)(2,1)}), bf16[128,56,128]{2,1,0:T(8,128)(2,1)}, u32[]{:S(2)}, u32[]{:S(2)}) %all-to-all-start.2) | async-done | bytes 1835040 | tf_op jit(solution)/shard_map/all_to_all | solution.py:372
  265.9 3.4 %copy.35 = f32[2,2,5,32,5,2,80]{6,5,4,3,1,2,0:T(2,128)} copy(f32[2,2,5,32,5,2,80]{6,5,0,3,1,4,2:T(2,128)S(1)} %bitcast.60) | data formatting | bytes 4096000 | tf_op jit(solution)/shard_map/mul | solution.py:390
  269.3 8.9 %mul.49 = f32[2,2,5,25600]{3,1,2,0:T(2,128)} reshape(f32[2,2,5,32,5,2,80]{6,5,4,3,1,2,0:T(2,128)} %copy.35) | data formatting | bytes 4096000 | tf_op jit(solution)/shard_map/mul | solution.py:390
  278.2 3.9 %sub.62 = f32[2,2,5,25600]{3,1,2,0:T(2,128)} subtract(f32[2,2,5,25600]{3,1,2,0:T(2,128)S(1)} %copy-done.9, f32[2,2,5,25600]{3,1,2,0:T(2,128)} %mul.49) | non-fusion elementwise | flops 512000 | bytes 6144000 | tf_op jit(solution)/shard_map/sub | solution.py:390
  (52 shorter events, 21.9 us)
Async XLA Ops:
  14.3 65.4 %all-to-all-start.1 = ((bf16[128,75,128]{2,1,0:T(8,128)(2,1)}), bf16[128,75,128]{2,1,0:T(8,128)(2,1)}, u32[]{:S(2)}, u32[]{:S(2)}) async-start(bf16[128,75,128]{2,1,0:T(8,128)(2,1)} %bitcast.16), calls=%async_computation.1 | async-start | bytes 5242880 | tf_op jit(solution)/shard_map/all_to_all | solution.py:358
  29.8 8.1 %copy-start.10 = (s32[2,2048]{1,0:T(2,128)S(1)}, s32[2,2048]{1,0:T(2,128)}, u32[]{:S(2)}) copy-start(s32[2,2048]{1,0:T(2,128)} %param.17) | copy-start | bytes 49156
  29.9 8.1 %copy-start.11 = (s32[2,2048]{1,0:T(2,128)S(1)}, s32[2,2048]{1,0:T(2,128)}, u32[]{:S(2)}) copy-start(s32[2,2048]{1,0:T(2,128)} %param.16) | copy-start | bytes 49156
  29.9 8.1 %copy-start.12 = (s32[2,1]{0,1:T(1,128)S(1)}, s32[2,1]{0,1:T(1,128)}, u32[]{:S(2)}) copy-start(s32[2,1]{0,1:T(1,128)} %param.18) | copy-start | bytes 28
  30.1 1.2 copy-start.8
  32.1 149.3 %collective-permute-start = (bf16[2,2,1,160,160]{4,3,1,2,0:T(8,128)(2,1)}, bf16[2,2,1,160,160]{4,3,1,2,0:T(8,128)(2,1)}, u32[]{:S(2)}, u32[]{:S(2)}) collective-permute-start(bf16[2,2,1,160,160]{4,3,1,2,0:T(8,128)(2,1)} %get-tuple-element.7), channel_id=1, source_target_pairs={{0,4},{4,8},{8,12},{12,16},{16,20},{20,24},{24,28},{28,32},{32,36}... | collective-permute-start | bytes 614408 | tf_op jit(solution)/shard_map/ppermute | solution.py:308
  35.8 145.6 %collective-permute-start.1 = (bf16[2,2,1,160,160]{4,3,1,2,0:T(8,128)(2,1)}, bf16[2,2,1,160,160]{4,3,1,2,0:T(8,128)(2,1)}, u32[]{:S(2)}, u32[]{:S(2)}) collective-permute-start(bf16[2,2,1,160,160]{4,3,1,2,0:T(8,128)(2,1)} %get-tuple-element.8), channel_id=1, source_target_pairs={{4,0},{8,4},{12,8},{16,12},{20,16},{24,20},{28,24},{32,28},{36,32}... | collective-permute-start | bytes 614408 | tf_op jit(solution)/shard_map/ppermute | solution.py:311
  79.6 138.5 %all-to-all-start = ((bf16[128,128,128]{2,1,0:T(8,128)(2,1)}), bf16[128,128,128]{2,1,0:T(8,128)(2,1)}, u32[]{:S(2)}, u32[]{:S(2)}) async-start(bf16[128,128,128]{2,1,0:T(8,128)(2,1)} %bitcast.64), calls=%async_computation | async-start | bytes 8388608 | tf_op jit(solution)/shard_map/all_to_all | solution.py:370
  173.4 1.4 copy-start.4
  175.2 4.0 %copy-start.6 = (f32[2,5,160,160]{3,2,1,0:T(8,128)}, f32[2,5,160,160]{3,2,1,0:T(8,128)S(1)}, u32[]{:S(2)}) copy-start(f32[2,5,160,160]{3,2,1,0:T(8,128)S(1)} %fusion.26) | copy-start | bytes 3072004
  183.6 3.3 %copy-start = (f32[2,2,7,160,160]{4,3,1,2,0:T(8,128)}, f32[2,2,7,160,160]{4,3,1,2,0:T(8,128)S(1)}, u32[]{:S(2)}) copy-start(f32[2,2,7,160,160]{4,3,1,2,0:T(8,128)S(1)} %maximum_convert_fusion) | copy-start | bytes 8601604
  231.3 32.8 %all-to-all-start.2 = ((bf16[128,56,128]{2,1,0:T(8,128)(2,1)}), bf16[128,56,128]{2,1,0:T(8,128)(2,1)}, u32[]{:S(2)}, u32[]{:S(2)}) async-start(bf16[128,56,128]{2,1,0:T(8,128)(2,1)} %bitcast.66), calls=%async_computation.2 | async-start | bytes 3670016 | tf_op jit(solution)/shard_map/all_to_all | solution.py:372
  236.2 3.5 %copy-start.1 = (f32[2,2,7,160,160]{4,3,1,2,0:T(8,128)S(1)}, f32[2,2,7,160,160]{4,3,1,2,0:T(8,128)}, u32[]{:S(2)}) copy-start(f32[2,2,7,160,160]{4,3,1,2,0:T(8,128)} %copy-done) | copy-start | bytes 8601604
  239.6 1.9 copy-start.2
  239.7 2.9 %copy-start.3 = (f32[2,2,5,160,160]{4,3,1,2,0:T(8,128)S(1)}, f32[2,2,5,160,160]{4,3,1,2,0:T(8,128)}, u32[]{:S(2)}) copy-start(f32[2,2,5,160,160]{4,3,1,2,0:T(8,128)} %get-tuple-element.10) | copy-start | bytes 6144004
  239.7 3.4 %copy-start.5 = (f32[1,2,5,160,160]{4,3,1,2,0:T(8,128)S(1)}, f32[1,2,5,160,160]{4,3,1,2,0:T(8,128)}, u32[]{:S(2)}) copy-start(f32[1,2,5,160,160]{4,3,1,2,0:T(8,128)} %sub.54) | copy-start | bytes 3072004
  239.7 3.8 %copy-start.7 = (f32[2,5,160,160]{3,2,1,0:T(8,128)S(1)}, f32[2,5,160,160]{3,2,1,0:T(8,128)}, u32[]{:S(2)}) copy-start(f32[2,5,160,160]{3,2,1,0:T(8,128)} %copy-done.6) | copy-start | bytes 3072004
  239.7 4.3 %slice-start = ((f32[2,2,5,160,160]{4,3,1,2,0:T(8,128)}), f32[1,2,5,160,160]{4,3,1,2,0:T(8,128)S(1)}, s32[]{:S(2)}) async-start(f32[2,2,5,160,160]{4,3,1,2,0:T(8,128)} %pad_divide_fusion), calls=%async_computation.3 | async-start | bytes 3276800 | tf_op jit(solution)/shard_map/slice | solution.py:328
  269.3 8.9 %copy-start.9 = (f32[2,2,5,25600]{3,1,2,0:T(2,128)S(1)}, f32[2,2,5,25600]{3,1,2,0:T(2,128)}, u32[]{:S(2)}) copy-start(f32[2,2,5,25600]{3,1,2,0:T(2,128)} %reshape.78) | copy-start | bytes 6144004
